TPU v7x, 256 devices: a whole 4x4x8 slice. The times are simulated.
256 devices in a mesh: docs: 2 (over y_hi), ctx: 8 (over z), mp: 16 (over y_lo, x, core).
Axes of the slice: x: 4, y: 4 (y_hi: 2, y_lo: 2; y = y_hi * 2 + y_lo), z: 8, core: 2. Of those that a mesh axis runs over, the one named last changes fastest.
Arguments:
- residual_in: bfloat16 [8192, 5376], P(('docs', 'ctx', 'mp')), parts along dimension 0, may hold values from -15 to 15
- document_start: int32 [8192], P(('docs', 'ctx')), parts along dimension 0, may hold values from 0 to 3584, as said below
- input_gain: float32 [5376], replicated, may hold values from 0.25 to 1.75
- query_weight: bfloat16 [5376, 4096], P(None, 'mp'), may hold values from -0.078125 to 0.078125
- key_weight: bfloat16 [5376, 2048], P(None, 'mp'), may hold values from -0.078125 to 0.078125
- value_weight: bfloat16 [5376, 2048], P(None, 'mp'), may hold values from -0.078125 to 0.078125
- query_gain: float32 [128], replicated, may hold values from 0.6 to 20
- key_gain: float32 [128], replicated, may hold values from 0.6 to 20
- output_weight: bfloat16 [4096, 5376], P('mp'), may hold values from -0.09375 to 0.09375
- post_gain: float32 [5376], replicated, may hold values from 0.25 to 1.75
Outputs:
- residual_out: bfloat16 [8192, 5376], P(('docs', 'ctx', 'mp')), parts along dimension 0
There are 2 independent parts, one for each index of `docs`. A program takes and returns all parts, laid end to end along the dimension named above; an argument that names none is the same for every part. Nothing has to cross between parts.
Inputs may be any that keep to these rules, and one draw needn't show every extreme that they name: `document_start`: each entry is the index of the first token of that token's document; the documents lie end to end, there are 4 of them, one has exactly 3072 tokens, and the last has exactly 512 tokens.
All inputs are finite; a program needn't handle non-finite values.
Results may differ from a plain program's by a relative error of at most 0.014.
The roundings to bfloat16 on the way count: a program that leaves them out, or rounds other values in their place, can miss the bound.
Values may be sent and summed in bfloat16 or wider, within the bound.
No kernel may reach another device: no remote copies, remote signals or barrier semaphores. Data moves between devices by JAX's collectives and lax.ppermute only.
A program may use at most 64 MiB of HBM per device.

v0:
```python
import math
import jax
import jax.numpy as jnp
from jax import lax
from jax.sharding import PartitionSpec as P

query_scalar = 168.0
rope_base = 1000000.0
rope_factor = 8.0
epsilon = 1e-06


def make_angles(positions, head_size):
    frequency = rope_base ** (-(jnp.arange(head_size // 2, dtype=jnp.float32) * 2.0 / head_size))
    return (positions.astype(jnp.float32) / rope_factor)[:, None] * frequency[None, :]


def norm_rotate(values, head_gain, angles, head_count):
    tokens_here = values.shape[0]
    head_size = head_gain.shape[0]
    shaped = values.reshape(tokens_here, head_count, head_size)
    scaled = (
        shaped * lax.rsqrt(jnp.mean(shaped * shaped, axis=-1, keepdims=True) + epsilon) * head_gain
    )
    half_size = head_size // 2
    first_half = scaled[..., :half_size]
    second_half = scaled[..., half_size:]
    cosine = jnp.cos(angles)[:, None, :]
    sine_values = jnp.sin(angles)[:, None, :]
    rotated = jnp.concatenate(
        [
            first_half * cosine - second_half * sine_values,
            second_half * cosine + first_half * sine_values,
        ],
        axis=-1,
    )
    return rotated.astype(jnp.bfloat16)


def block_step(query_block, carried, key_piece, value_piece, key_index, first_row, piece_rows):
    queries, query_index, query_start = query_block

    def compute(running):
        running_max, running_total, accumulated = running
        scores = jnp.einsum(
            "tkgd,nkd->tkgn", queries, key_piece, preferred_element_type=jnp.float32
        ) / math.sqrt(query_scalar)
        allowed = (key_index[None, :] >= query_start[:, None]) & (
            key_index[None, :] <= query_index[:, None]
        )
        allowed = allowed[:, None, None, :]
        masked = jnp.where(allowed, scores, -1e30)
        new_max = jnp.maximum(running_max, jnp.max(masked, axis=-1))
        weights = jnp.where(allowed, jnp.exp(masked - new_max[..., None]), 0.0)
        new_total = jnp.sum(weights, axis=-1)
        product = jnp.einsum(
            "tkgn,nkd->tkgd",
            weights.astype(jnp.bfloat16),
            value_piece,
            preferred_element_type=jnp.float32,
        )
        return (new_max, new_total, product)

    def keep(running):
        return running

    is_live = (first_row <= jnp.max(query_index)) & (
        first_row + piece_rows - 1 >= jnp.min(query_start)
    )
    return lax.cond(is_live, compute, keep, carried)


def attend(query_blocks, key_rows, value_rows):
    initial = []
    for query_block in query_blocks:
        query_rows, kv_count, group_size, head_size = query_block[0].shape
        initial.append(
            (
                jnp.full((query_rows, kv_count, group_size), -1e30, jnp.float32),
                jnp.zeros((query_rows, kv_count, group_size), jnp.float32),
                jnp.zeros((query_rows, kv_count, group_size, head_size), jnp.float32),
            )
        )
    carried = tuple(initial)
    first_row = jnp.int32(0)
    key_piece = lax.all_gather(key_rows, "ctx", axis=0, tiled=True)
    value_piece = lax.all_gather(value_rows, "ctx", axis=0, tiled=True)
    piece_rows = key_piece.shape[0]
    key_index = jnp.arange(piece_rows, dtype=jnp.int32)
    outcome = []
    for query_block, carry_block in zip(query_blocks, carried):
        outcome.append(
            block_step(
                query_block, carry_block, key_piece, value_piece, key_index, first_row, piece_rows
            )
        )
    finals = tuple(outcome)
    results = []
    for final_block in finals:
        running_max, running_total, accumulated = final_block
        query_rows = accumulated.shape[0]
        results.append(
            (accumulated / running_total[..., None]).reshape(query_rows, -1).astype(jnp.bfloat16)
        )
    return results[0]


def body(
    residual_in,
    document_start,
    input_gain,
    query_weight,
    key_weight,
    value_weight,
    query_gain,
    key_gain,
    output_weight,
    post_gain,
):
    head_size = query_gain.shape[0]
    gathered = lax.all_gather(residual_in, "mp", axis=0, tiled=True)
    local_tokens = gathered.shape[0]
    widened = gathered.astype(jnp.float32)
    normed = (
        widened
        * lax.rsqrt(jnp.mean(widened * widened, axis=-1, keepdims=True) + epsilon)
        * input_gain
    ).astype(jnp.bfloat16)
    query_raw = jnp.dot(normed, query_weight, preferred_element_type=jnp.float32)
    key_raw = jnp.dot(normed, key_weight, preferred_element_type=jnp.float32)
    value_rows = jnp.dot(normed, value_weight, preferred_element_type=jnp.float32).astype(
        jnp.bfloat16
    )
    query_count = query_weight.shape[1] // head_size
    kv_count = key_weight.shape[1] // head_size
    group_size = query_count // kv_count
    block_index = lax.axis_index("ctx")
    positions = block_index * local_tokens + jnp.arange(local_tokens, dtype=jnp.int32)
    angles = make_angles(positions - document_start, head_size)
    query_rot = norm_rotate(query_raw, query_gain, angles, query_count).reshape(
        local_tokens, kv_count, group_size, head_size
    )
    key_rot = norm_rotate(key_raw, key_gain, angles, kv_count)
    value_heads = value_rows.reshape(local_tokens, kv_count, head_size)
    attended = attend([(query_rot, positions, document_start)], key_rot, value_heads)
    summed = lax.psum_scatter(
        jnp.dot(attended, output_weight, preferred_element_type=jnp.float32).astype(jnp.bfloat16),
        "mp",
        scatter_dimension=0,
        tiled=True,
    ).astype(jnp.float32)
    branch = (
        summed * lax.rsqrt(jnp.mean(summed * summed, axis=-1, keepdims=True) + epsilon) * post_gain
    )
    return (residual_in.astype(jnp.float32) + branch).astype(jnp.bfloat16)


def solution(mesh):
    return jax.shard_map(
        body,
        mesh=mesh,
        in_specs=(
            P(("docs", "ctx", "mp"), None),
            P(("docs", "ctx")),
            P(),
            P(None, "mp"),
            P(None, "mp"),
            P(None, "mp"),
            P(),
            P(),
            P("mp", None),
            P(),
        ),
        out_specs=P(("docs", "ctx", "mp"), None),
        check_vma=False,
    )
```

profile of v0, /device:TPU:32, one launch (start us, length us, event | category | flops | bytes accessed | tf_op | source)
XLA Modules:
  0.0 245.3 jit_solution(6276417553406046301)
XLA Ops:
  6.5 0.7 all-gather.5.cloned.1.call-update
  7.3 47.2 %all-gather.5.cloned.1.call-done = bf16[512,5376]{1,0:T(8,128)(2,1)} async-done(((bf16[32,5376]{1,0:T(8,128)(2,1)}), bf16[512,5376]{1,0:T(8,128)(2,1)}) %all-gather.5.cloned.1.call-update) | async-done | bytes 5505040 | tf_op jit(solution)/shard_map/all_gather | solution.py:121
  54.5 3.9 %fusion.17 = f32[512]{0:T(512)S(1)} fusion(bf16[512,5376]{1,0:T(8,128)(2,1)} %all-gather.5.cloned.1.call-done), kind=kLoop, calls=%fused_computation.20 | loop fusion | flops 8257024 | bytes 5507072 | tf_op jit(solution)/shard_map/reduce_sum | solution.py:126
  58.6 1.9 fusion.19
  60.5 2.4 copy-done.1
  62.9 2.3 convolution_convert_fusion.1
  65.3 4.9 %multiply_reduce_fusion.1 = (f32[512]{0:T(512)S(1)}, f32[512,128]{0,1:T(8,128)S(1)}) fusion(bf16[512,5376]{1,0:T(8,128)(2,1)} %copy-done.1, bf16[5376,128]{1,0:T(8,128)(2,1)} %param.16), kind=kOutput, calls=%fused_computation.42 | convolution fusion | flops 704773632 | bytes 7145472 | tf_op jit(solution)/shard_map/dot_general | solution.py:130
  70.9 0.7 pad_maximum_fusion.1
  72.3 0.7 reduce_min.9
  74.9 1.7 multiply_cosine_fusion
  76.6 5.9 %multiply_reduce_fusion = (f32[512,2]{0,1:T(2,128)S(1)}, f32[512,256]{0,1:T(8,128)}) fusion(bf16[512,5376]{1,0:T(8,128)(2,1)} %copy-done.1, bf16[5376,256]{1,0:T(8,128)(2,1)} %param.15), kind=kOutput, calls=%fused_computation.35 | convolution fusion | flops 1409547264 | bytes 8785920 | tf_op jit(solution)/shard_map/dot_general | solution.py:129
  82.5 1.2 copy.21
  83.9 1.2 fusion.24
  85.3 17.8 %all-gather.9.cloned.1.call-done = bf16[4096,128]{1,0:T(8,128)(2,1)} async-done(((bf16[512,128]{1,0:T(8,128)(2,1)}), bf16[4096,128]{1,0:T(8,128)(2,1)}) %all-gather.9.cloned.1.call-update) | async-done | bytes 1048592 | tf_op jit(solution)/shard_map/all_gather | solution.py:87
  103.1 39.0 %all-gather.7.cloned.1.call-done = bf16[4096,1,128]{0,2,1:T(8,128)(2,1)} async-done(((bf16[512,1,128]{0,2,1:T(8,128)(2,1)}), bf16[4096,1,128]{0,2,1:T(8,128)(2,1)}) %all-gather.7.cloned.1.call-update) | async-done | bytes 1048592 | tf_op jit(solution)/shard_map/all_gather | solution.py:86
  142.2 18.4 %conditional.1 = (f32[512,1,2]{0,2,1:T(2,128)S(1)}, f32[512,1,2,128]{0,3,2,1:T(8,128)S(1)}) conditional(s32[]{:T(128)} %convert_element_type.54, () %tuple.13, (s32[4096]{0:T(1024)S(1)}, s32[4096]{0:T(1024)S(1)}, s32[512]{0:T(512)}, s32[512]{0:T(512)}, bf16[4096,1,128]{0,2,1:T(8,128)(2,1)}, /*index=5*/bf16[512,1,2,128]{3,0,2,1:T(8,128)(2,1)S(1)}, ...), branch_computations={%region_5.0_spmd, %region_6.9_spmd} | conditional | flops 2208300032 | bytes 65859628 | solution.py:70
  142.2 3.8 %compare_and_fusion = pred[512,4096]{0,1:T(8,128)(4,1)S(1)} fusion(s32[512]{0:T(512)} %get-tuple-element.21, s32[512]{0:T(512)} %get-tuple-element.19, s32[4096]{0:T(1024)S(1)} %get-tuple-element.20, s32[4096]{0:T(1024)S(1)} %get-tuple-element.20), kind=kLoop, calls=%fused_computation.8 | loop fusion | flops 6291456 | bytes 2134016 | tf_op jit(solution)/shard_map/cond/branch_1_fun/and | solution.py:48
  146.0 5.2 %fusion = (f32[512,2]{0,1:T(2,128)S(1)}, f32[4096,512,2]{1,0,2:T(8,128)S(1)}) fusion(pred[512,4096]{0,1:T(8,128)(4,1)S(1)} %compare_and_fusion, bf16[512,1,2,128]{3,0,2,1:T(8,128)(2,1)S(1)} %get-tuple-element.23, bf16[4096,1,128]{0,2,1:T(8,128)(2,1)} %get-tuple-element.47), kind=kOutput, calls=%fused_computation.2 | convolution fusion | flops 1086323712 | bytes 20189184 | tf_op jit(solution)/shard_map/cond/branch_1_fun/tkgd,nkd->tkgn/dot_general | solution.py:45
  151.2 5.0 %fusion.7 = f32[512,1,2,128]{0,3,2,1:T(8,128)S(1)} fusion(f32[4096,512,2]{1,0,2:T(8,128)S(1)} %get-tuple-element.52, f32[512,2]{0,1:T(2,128)S(1)} %broadcast_maximum_fusion, pred[512,4096]{0,1:T(8,128)(4,1)S(1)} %compare_and_fusion, bf16[4096,1,128]{2,0,1:T(8,128)(2,1)S(1)} %copy-done.10), kind=kOutput, calls=%fused_computation.9 | convolution fusion | flops 1094713344 | bytes 20451328 | tf_op jit(solution)/shard_map/cond/branch_1_fun/tkgn,nkd->tkgd/dot_general | solution.py:56
  156.1 4.4 %fusion.2 = f32[512,2]{0,1:T(2,128)S(1)} fusion(f32[4096,512,2]{1,0,2:T(8,128)S(1)} %get-tuple-element.52, f32[512,2]{0,1:T(2,128)S(1)} %broadcast_maximum_fusion, pred[512,4096]{0,1:T(8,128)(4,1)S(1)} %compare_and_fusion), kind=kLoop, calls=%fused_computation.4 | loop fusion | flops 20970496 | bytes 18882560 | tf_op jit(solution)/shard_map/cond/branch_1_fun/reduce_sum | solution.py:55
  160.7 4.0 %convolution_convert_fusion = bf16[512,5376]{1,0:T(8,128)(2,1)} fusion(bf16[512,256]{0,1:T(8,128)(2,1)S(1)} %bitcast.65, bf16[256,5376]{1,0:T(8,128)(2,1)S(1)} %copy-done), kind=kOutput, calls=%fused_computation.23 | convolution fusion | flops 1412038656 | bytes 8519680 | tf_op jit(solution)/shard_map/dot_general | solution.py:147
  164.8 70.9 %reduce-scatter.2.cloned.1.call-done = bf16[32,5376]{1,0:T(8,128)(2,1)} async-done(((bf16[512,5376]{1,0:T(8,128)(2,1)}), bf16[32,5376]{1,0:T(8,128)(2,1)}) %reduce-scatter.2.cloned.1.call-update) | async-done | bytes 344080 | tf_op jit(solution)/shard_map/reduce_scatter | solution.py:146
  235.7 1.2 fusion.20
  236.9 1.9 fusion.23
  (43 shorter events, 2.9 us)
Async XLA Ops:
  6.5 154.1 %copy-start = (bf16[256,5376]{1,0:T(8,128)(2,1)S(1)}, bf16[256,5376]{1,0:T(8,128)(2,1)}, u32[]{:S(2)}) copy-start(bf16[256,5376]{1,0:T(8,128)(2,1)} %param.20) | copy-start | bytes 8257540
  6.5 51.8 %copy-start.5 = (f32[5376]{0:T(1024)S(1)}, f32[5376]{0:T(1024)}, u32[]{:S(2)}) copy-start(f32[5376]{0:T(1024)} %param.14) | copy-start | bytes 64516
  6.5 47.9 %all-gather.5.cloned.1.call-start = ((), (), s32[]{:S(2)}) async-start(), calls=%async_computation.1 | async-start | bytes 5849088 | tf_op jit(solution)/shard_map/all_gather | solution.py:121
  7.3 95.9 %all-gather.9.cloned.1.call-start = ((), (), s32[]{:S(2)}) async-start(), calls=%async_computation.4 | async-start | bytes 1179648 | tf_op jit(solution)/shard_map/all_gather | solution.py:87
  54.5 4.2 %copy-start.2 = (bf16[512,5376]{1,0:T(8,128)(2,1)S(1)}, bf16[512,5376]{1,0:T(8,128)(2,1)}, u32[]{:S(2)}) copy-start(bf16[512,5376]{1,0:T(8,128)(2,1)} %all-gather.5.cloned.1.call-done) | copy-start | bytes 16515076
  58.6 4.3 %copy-start.9 = (bf16[5376,128]{1,0:T(8,128)(2,1)S(1)}, bf16[5376,128]{1,0:T(8,128)(2,1)}, u32[]{:S(2)}) copy-start(bf16[5376,128]{1,0:T(8,128)(2,1)} %param.17) | copy-start | bytes 4128772
  60.5 2.4 copy-start.1
  62.9 2.4 copy-start.6
  65.2 5.1 %copy-start.7 = (f32[128]{0:T(128)S(1)}, f32[128]{0:T(128)}, u32[]{:S(2)}) copy-start(f32[128]{0:T(128)} %param.19) | copy-start | bytes 1540
  65.2 77.0 %all-gather.7.cloned.1.call-start = ((), (), s32[]{:S(2)}) async-start(), calls=%async_computation.2 | async-start | bytes 1179648 | tf_op jit(solution)/shard_map/all_gather | solution.py:86
  71.6 164.1 %reduce-scatter.2.cloned.1.call-start = ((), (), s32[]{:S(2)}) async-start(), calls=%async_computation.3 | async-start | bytes 5849088 | tf_op jit(solution)/shard_map/reduce_scatter | solution.py:146
  76.6 7.1 %copy-start.8 = (f32[128]{0:T(128)S(1)}, f32[128]{0:T(128)}, u32[]{:S(2)}) copy-start(f32[128]{0:T(128)} %param.18) | copy-start | bytes 1540
  146.0 5.2 %copy-start.10 = (bf16[4096,1,128]{2,0,1:T(8,128)(2,1)S(1)}, bf16[4096,1,128]{2,0,1:T(8,128)(2,1)}, u32[]{:S(2)}) copy-start(bf16[4096,1,128]{2,0,1:T(8,128)(2,1)} %get-tuple-element.24) | copy-start | bytes 3145732 | tf_op jit(solution)/shard_map/cond
  160.7 76.2 %copy-start.3 = (bf16[32,5376]{1,0:T(8,128)(2,1)S(1)}, bf16[32,5376]{1,0:T(8,128)(2,1)}, u32[]{:S(2)}) copy-start(bf16[32,5376]{1,0:T(8,128)(2,1)} %param.12) | copy-start | bytes 1032196
  160.7 76.2 %copy-start.4 = (f32[5376]{0:T(1024)S(1)}, f32[5376]{0:T(1024)}, u32[]{:S(2)}) copy-start(f32[5376]{0:T(1024)} %param.21) | copy-start | bytes 64516
Sparse Core Ops, SparseCore 0:
  9.2 45.2 all-gather.4
  65.3 37.7 all-gather.8
  104.9 37.1 all-gather.6
  164.9 70.7 reduce-scatter.1
where the time goes:
time: 246 us; the launch traced here: 245 us
  waiting for transfers between devices  176 us (72%)
  matrix products  27.2 us (11%)
  other arithmetic  23.6 us (10%)
  between operations  14.6 us (6%)
  local copies, waits for them, and re-layouts  3.97 us (2%)
    reduce_scatter x1, waiting for transfers between devices, body(): lax.psum_scatter(jnp.dot(attended, output_weight, preferred_element_type=...  70.9 us
    all_gather x1, waiting for transfers between devices, body(): gathered = lax.all_gather(residual_in, 'mp', axis=0, tiled=True)  47.2 us
    all_gather x1, waiting for transfers between devices, attend(): key_piece = lax.all_gather(key_rows, 'ctx', axis=0, tiled=True)  39 us
    all_gather x1, waiting for transfers between devices, attend(): value_piece = lax.all_gather(value_rows, 'ctx', axis=0, tiled=True)  17.8 us
    dot_general x1, matrix products, body(): jnp.dot(normed, query_weight, preferred_element_type=jnp.float32)  5.87 us
    dot_general x1, matrix products, compute(): jnp.einsum('tkgd,nkd->tkgn', queries, key_piece, preferred_element_type=j...  5.17 us
    dot_general x1, matrix products, compute(): jnp.einsum('tkgn,nkd->tkgd', weights.astype(jnp.bfloat16), value_piece, p...  4.97 us
    dot_general x1, matrix products, body(): key_raw = jnp.dot(normed, key_weight, preferred_element_type=jnp.float32)  4.92 us
  transfers between devices with their start and end apart: 4, of which 4 were waited for; matrix products, arithmetic and copies ran while one was open for 8% of the time, Pallas kernels for 0%

commit v1 on v0

--- a/solution.py
+++ b/solution.py
@@ -83,7 +83,16 @@
         )
     carried = tuple(initial)
     first_row = jnp.int32(0)
-    key_piece = lax.all_gather(key_rows, "ctx", axis=0, tiled=True)
+    ways = lax.axis_size("ctx")
+    up = [(d, (d + 1) % ways) for d in range(ways)]
+    down = [(d, (d - 1) % ways) for d in range(ways)]
+    earlier, later = ([key_rows], [key_rows])
+    for _ in range(ways // 2):
+        earlier.append(lax.ppermute(earlier[-1], "ctx", up))
+    for _ in range((ways - 1) // 2):
+        later.append(lax.ppermute(later[-1], "ctx", down))
+    line = jnp.concatenate([*earlier[::-1], *later[1:]], axis=0)
+    key_piece = jnp.roll(line, (lax.axis_index("ctx") - ways // 2) * key_rows.shape[0], axis=0)
     value_piece = lax.all_gather(value_rows, "ctx", axis=0, tiled=True)
     piece_rows = key_piece.shape[0]
     key_index = jnp.arange(piece_rows, dtype=jnp.int32)

time: 246 us -> 222 us (0.902)
  waiting for transfers between devices: 176 us -> 126 us
  local copies, waits for them, and re-layouts: 3.97 us -> 16.9 us
  starting transfers between devices: 0.13 us -> 9.77 us
  other arithmetic: 23.6 us -> 29.6 us
  matrix products: 27.2 us -> 24.5 us
    all_gather x1 -> x0, waiting for transfers between devices: 39 us -> none  [attend(): key_piece = lax.all_gather(key_rows, 'ctx', axis=0, tiled=True)]
    all_gather x1, waiting for transfers between devices: 17.8 us -> 0.01 us  [attend(): value_piece = lax.all_gather(value_rows, 'ctx', axis=0, tiled=True)]
    ppermute x0 -> x7, waiting for transfers between devices: none -> 10.7 us  [the longest x4 10.7 us: attend(): earlier.append(lax.ppermute(earlier[-1], 'ctx', up))]
    ppermute x0 -> x7, starting transfers between devices: none -> 9.68 us  [the longest x4 8.12 us: attend(): earlier.append(lax.ppermute(earlier[-1], 'ctx', up))]
    unnamed x20 -> x33, local copies, waits for them, and re-layouts: 2.73 us -> 10.9 us
    all_gather x1, waiting for transfers between devices: 47.2 us -> 40.8 us  [body(): gathered = lax.all_gather(residual_in, 'mp', axis=0, tiled=True)]
    another operation x0 -> x1, local copies, waits for them, and re-layouts: none -> 4.06 us
    dot_general x1, matrix products: 4.92 us -> 1.96 us  [body(): key_raw = jnp.dot(normed, key_weight, preferred_element_type=jnp.float32)]
  transfers between devices with their start and end apart: 4 -> 10, of which waited for: 4 -> 5; matrix products, arithmetic and copies ran while one was open for 8% -> 13% of each run, Pallas kernels for 0% -> 0%
where the time goes in v1:
time: 222 us; the launch traced here: 221 us
  waiting for transfers between devices  126 us (57%)
  other arithmetic  29.6 us (13%)
  matrix products  24.5 us (11%)
  local copies, waits for them, and re-layouts  16.9 us (8%)
  between operations  14.6 us (7%)
  starting transfers between devices  9.77 us (4%)
    reduce_scatter x1, waiting for transfers between devices, body(): lax.psum_scatter(jnp.dot(attended, output_weight, preferred_element_type=...  73.5 us
    all_gather x1, waiting for transfers between devices, body(): gathered = lax.all_gather(residual_in, 'mp', axis=0, tiled=True)  40.8 us
    unnamed x33, local copies, waits for them, and re-layouts  10.9 us
    ppermute x4, waiting for transfers between devices, attend(): earlier.append(lax.ppermute(earlier[-1], 'ctx', up))  10.7 us
    ppermute x4, starting transfers between devices, attend(): earlier.append(lax.ppermute(earlier[-1], 'ctx', up))  8.12 us
    dot_general x1, matrix products, body(): jnp.dot(normed, query_weight, preferred_element_type=jnp.float32)  5.85 us
    dot_general x1, matrix products, compute(): jnp.einsum('tkgd,nkd->tkgn', queries, key_piece, preferred_element_type=j...  5.42 us
    reduce_sum x1, other arithmetic, compute(): new_total = jnp.sum(weights, axis=-1)  5.04 us
  transfers between devices with their start and end apart: 10, of which 5 were waited for; matrix products, arithmetic and copies ran while one was open for 13% of the time, Pallas kernels for 0%

profile of v1, /device:TPU:32, one launch (start us, length us, event | category | flops | bytes accessed | tf_op | source)
XLA Modules:
  0.0 221.1 jit_solution(4326394822888449590)
XLA Ops:
  11.9 1.8 multiply_cosine_fusion
  13.7 40.8 %all-gather.4.cloned.1.call-done = bf16[512,5376]{1,0:T(8,128)(2,1)} async-done(((bf16[32,5376]{1,0:T(8,128)(2,1)}), bf16[512,5376]{1,0:T(8,128)(2,1)}) %all-gather.4.cloned.1.call-update) | async-done | bytes 5505040 | tf_op jit(solution)/shard_map/all_gather | solution.py:130
  54.5 3.9 %fusion.19 = f32[512]{0:T(512)S(1)} fusion(bf16[512,5376]{1,0:T(8,128)(2,1)} %all-gather.4.cloned.1.call-done), kind=kLoop, calls=%fused_computation.22 | loop fusion | flops 8257024 | bytes 5507072 | tf_op jit(solution)/shard_map/reduce_sum | solution.py:135
  58.6 1.9 fusion.21
  60.6 2.0 multiply_reduce_fusion.1
  65.9 2.2 %convolution_convert_fusion.1 = bf16[512,128]{1,0:T(8,128)(2,1)} fusion(bf16[512,5376]{1,0:T(8,128)(2,1)S(1)} %fusion.21, bf16[5376,128]{1,0:T(8,128)(2,1)S(1)} %copy-done.11), kind=kOutput, calls=%fused_computation.26 | convolution fusion | flops 704708608 | bytes 7012352 | tf_op jit(solution)/shard_map/dot_general | solution.py:140
  68.2 5.9 %multiply_reduce_fusion = (f32[512,2]{0,1:T(2,128)S(1)}, f32[512,256]{0,1:T(8,128)}) fusion(bf16[512,5376]{1,0:T(8,128)(2,1)} %copy-done.1, bf16[5376,256]{1,0:T(8,128)(2,1)} %param.15), kind=kOutput, calls=%fused_computation.37 | convolution fusion | flops 1409547264 | bytes 8785920 | tf_op jit(solution)/shard_map/dot_general | solution.py:138
  75.3 1.6 collective-permute-start.1
  77.0 5.4 %collective-permute-done.1 = bf16[512,1,128]{0,2,1:T(8,128)(2,1)S(1)} collective-permute-done((bf16[512,1,128]{0,2,1:T(8,128)(2,1)}, bf16[512,1,128]{0,2,1:T(8,128)(2,1)S(1)}, u32[]{:S(2)}, u32[]{:S(2)}) %collective-permute-start.1) | collective-permute-done | bytes 131104 | tf_op jit(solution)/shard_map/ppermute | solution.py:91
  82.4 2.5 %collective-permute-start.2 = (bf16[512,1,128]{0,2,1:T(8,128)(2,1)S(1)}, bf16[512,1,128]{0,2,1:T(8,128)(2,1)S(1)}, u32[]{:S(2)}, u32[]{:S(2)}) collective-permute-start(bf16[512,1,128]{0,2,1:T(8,128)(2,1)S(1)} %collective-permute-done.1), channel_id=1, source_target_pairs={{0,16},{16,32},{32,48},{48,64},{64,80},{80,96},{96,112},{112,0},{1... | collective-permute-start | bytes 393224 | tf_op jit(solution)/shard_map/ppermute | solution.py:91
  85.5 3.4 %collective-permute-done.2 = bf16[512,1,128]{0,2,1:T(8,128)(2,1)S(1)} collective-permute-done((bf16[512,1,128]{0,2,1:T(8,128)(2,1)S(1)}, bf16[512,1,128]{0,2,1:T(8,128)(2,1)S(1)}, u32[]{:S(2)}, u32[]{:S(2)}) %collective-permute-start.2) | collective-permute-done | bytes 131104 | tf_op jit(solution)/shard_map/ppermute | solution.py:91
  88.8 2.5 %collective-permute-start.3 = (bf16[512,1,128]{0,2,1:T(8,128)(2,1)S(1)}, bf16[512,1,128]{0,2,1:T(8,128)(2,1)S(1)}, u32[]{:S(2)}, u32[]{:S(2)}) collective-permute-start(bf16[512,1,128]{0,2,1:T(8,128)(2,1)S(1)} %collective-permute-done.2), channel_id=1, source_target_pairs={{0,16},{16,32},{32,48},{48,64},{64,80},{80,96},{96,112},{112,0},{1... | collective-permute-start | bytes 393224 | tf_op jit(solution)/shard_map/ppermute | solution.py:91
  94.1 1.9 collective-permute-done.3
  98.0 1.6 constant_dynamic-update-slice_fusion.12
  104.4 1.6 constant_dynamic-update-slice_fusion.4
  108.7 24.6 %conditional.1 = (f32[512,1,2]{0,2,1:T(2,128)}, f32[512,1,2,128]{0,3,2,1:T(8,128)S(1)}) conditional(s32[]{:T(128)} %convert_element_type.57, () %tuple.24, (s32[4096]{0:T(1024)S(1)}, s32[4096]{0:T(1024)S(1)}, s32[512]{0:T(512)}, s32[512]{0:T(512)}, s32[]{:T(128)}, /*index=5*/s32[]{:T(128)}, bf16[8192,1,128]{0,2,1:T(8,128)(2,1)}, ...), branch_computations={%region_5.6_spmd, %region_6.9_spmd} | conditional | flops 2208300032 | bytes 79491328 | solution.py:70
  108.7 5.0 %compare_and_fusion = pred[512,4096]{0,1:T(8,128)(4,1)} fusion(s32[512]{0:T(512)} %get-tuple-element.118, s32[512]{0:T(512)} %get-tuple-element.116, s32[4096]{0:T(1024)S(1)} %get-tuple-element.117, s32[4096]{0:T(1024)S(1)} %get-tuple-element.117), kind=kLoop, calls=%fused_computation.8 | loop fusion | flops 6291456 | bytes 2134016 | tf_op jit(solution)/shard_map/cond/branch_1_fun/and | solution.py:48
  113.7 4.1 %copy.22 = bf16[8192,1,128]{2,0,1:T(8,128)(2,1)} copy(bf16[8192,1,128]{0,2,1:T(8,128)(2,1)} %get-tuple-element.164) | data formatting | bytes 4194304 | tf_op jit(solution)/shard_map
  117.8 5.4 %fusion = (f32[512,2]{0,1:T(2,128)S(1)}, f32[4096,512,2]{1,0,2:T(8,128)S(1)}) fusion(pred[512,4096]{0,1:T(8,128)(4,1)} %compare_and_fusion, bf16[512,1,2,128]{3,0,2,1:T(8,128)(2,1)S(1)} %copy-done.6, bf16[8192,1,128]{2,0,1:T(8,128)(2,1)} %copy.22, s32[]{:T(128)S(6)} %select_n.30), kind=kOutput, calls=%fused_computation.2 | convolution fusion | flops 1086323712 | bytes 20189188 | tf_op jit(solution)/shard_map/cond/branch_1_fun/tkgd,nkd->tkgn/dot_general | solution.py:45
  123.2 5.0 %fusion.7 = f32[512,1,2,128]{0,3,2,1:T(8,128)S(1)} fusion(f32[4096,512,2]{1,0,2:T(8,128)S(1)} %get-tuple-element.174, f32[512,2]{0,1:T(2,128)S(1)} %broadcast_maximum_fusion, pred[512,4096]{0,1:T(8,128)(4,1)S(1)} %copy-done.3, bf16[4096,1,128]{2,0,1:T(8,128)(2,1)S(1)} %copy-done.12), kind=kOutput, calls=%fused_computation.9 | convolution fusion | flops 1094713344 | bytes 20451328 | tf_op jit(solution)/shard_map/cond/branch_1_fun/tkgn,nkd->tkgd/dot_general | solution.py:56
  128.2 5.0 %fusion.2 = f32[512,2]{0,1:T(2,128)} fusion(f32[4096,512,2]{1,0,2:T(8,128)S(1)} %get-tuple-element.174, f32[512,2]{0,1:T(2,128)S(1)} %broadcast_maximum_fusion, pred[512,4096]{0,1:T(8,128)(4,1)S(1)} %copy-done.3), kind=kLoop, calls=%fused_computation.4 | loop fusion | flops 20970496 | bytes 18882560 | tf_op jit(solution)/shard_map/cond/branch_1_fun/reduce_sum | solution.py:55
  134.0 4.1 %convolution_convert_fusion = bf16[512,5376]{1,0:T(8,128)(2,1)} fusion(bf16[512,256]{0,1:T(8,128)(2,1)S(1)} %bitcast.64, bf16[256,5376]{1,0:T(8,128)(2,1)S(1)} %copy-done), kind=kOutput, calls=%fused_computation.25 | convolution fusion | flops 1412038656 | bytes 8519680 | tf_op jit(solution)/shard_map/dot_general | solution.py:156
  138.1 73.5 %reduce-scatter.2.cloned.1.call-done = bf16[32,5376]{1,0:T(8,128)(2,1)} async-done(((bf16[512,5376]{1,0:T(8,128)(2,1)}), bf16[32,5376]{1,0:T(8,128)(2,1)}) %reduce-scatter.2.cloned.1.call-update) | async-done | bytes 344080 | tf_op jit(solution)/shard_map/reduce_scatter | solution.py:155
  212.7 1.9 fusion.25
  (75 shorter events, 23.8 us)
Async XLA Ops:
  6.5 127.4 %copy-start = (bf16[256,5376]{1,0:T(8,128)(2,1)S(1)}, bf16[256,5376]{1,0:T(8,128)(2,1)}, u32[]{:S(2)}) copy-start(bf16[256,5376]{1,0:T(8,128)(2,1)} %param.20) | copy-start | bytes 8257540
  6.5 47.9 %all-gather.4.cloned.1.call-start = ((), (), s32[]{:S(2)}) async-start(), calls=%async_computation.1 | async-start | bytes 5849088 | tf_op jit(solution)/shard_map/all_gather | solution.py:130
  7.3 101.4 %all-gather.6.cloned.1.call-start = ((), (), s32[]{:S(2)}) async-start(), calls=%async_computation.3 | async-start | bytes 1179648 | tf_op jit(solution)/shard_map/all_gather | solution.py:96
  11.9 46.5 %copy-start.8 = (f32[5376]{0:T(1024)S(1)}, f32[5376]{0:T(1024)}, u32[]{:S(2)}) copy-start(f32[5376]{0:T(1024)} %param.14) | copy-start | bytes 64516
  54.5 4.2 %copy-start.2 = (bf16[512,5376]{1,0:T(8,128)(2,1)S(1)}, bf16[512,5376]{1,0:T(8,128)(2,1)}, u32[]{:S(2)}) copy-start(bf16[512,5376]{1,0:T(8,128)(2,1)} %all-gather.4.cloned.1.call-done) | copy-start | bytes 16515076
  58.6 1.9 copy-start.5
  60.5 5.4 %copy-start.1 = (bf16[512,5376]{1,0:T(8,128)(2,1)}, bf16[512,5376]{1,0:T(8,128)(2,1)S(1)}, u32[]{:S(2)}) copy-start(bf16[512,5376]{1,0:T(8,128)(2,1)S(1)} %fusion.21) | copy-start | bytes 16515076
  60.5 2.0 copy-start.9
  60.6 5.3 %copy-start.11 = (bf16[5376,128]{1,0:T(8,128)(2,1)S(1)}, bf16[5376,128]{1,0:T(8,128)(2,1)}, u32[]{:S(2)}) copy-start(bf16[5376,128]{1,0:T(8,128)(2,1)} %param.17) | copy-start | bytes 4128772
  63.9 21.2 %collective-permute-start.4 = (bf16[512,1,128]{0,2,1:T(8,128)(2,1)}, bf16[512,1,128]{0,2,1:T(8,128)(2,1)S(1)}, u32[]{:S(2)}, u32[]{:S(2)}) collective-permute-start(bf16[512,1,128]{0,2,1:T(8,128)(2,1)} %pad_maximum_fusion.1), channel_id=1, source_target_pairs={{0,112},{16,0},{32,16},{48,32},{64,48},{80,64},{96,80},{112,96},{1... | collective-permute-start | bytes 393224 | tf_op jit(solution)/shard_map/ppermute | solution.py:93
  64.3 11.0 %collective-permute-start = (bf16[512,1,128]{0,2,1:T(8,128)(2,1)}, bf16[512,1,128]{0,2,1:T(8,128)(2,1)}, u32[]{:S(2)}, u32[]{:S(2)}) collective-permute-start(bf16[512,1,128]{0,2,1:T(8,128)(2,1)} %pad_maximum_fusion.1), channel_id=1, source_target_pairs={{0,16},{16,32},{32,48},{48,64},{64,80},{80,96},{96,112},{112,0},{1... | collective-permute-start | bytes 393224 | tf_op jit(solution)/shard_map/ppermute | solution.py:91
  68.2 16.7 %copy-start.10 = (f32[128]{0:T(128)S(1)}, f32[128]{0:T(128)}, u32[]{:S(2)}) copy-start(f32[128]{0:T(128)} %param.18) | copy-start | bytes 1540
  68.2 143.4 %reduce-scatter.2.cloned.1.call-start = ((), (), s32[]{:S(2)}) async-start(), calls=%async_computation.2 | async-start | bytes 5849088 | tf_op jit(solution)/shard_map/reduce_scatter | solution.py:155
  75.3 7.1 %collective-permute-start.1 = (bf16[512,1,128]{0,2,1:T(8,128)(2,1)}, bf16[512,1,128]{0,2,1:T(8,128)(2,1)S(1)}, u32[]{:S(2)}, u32[]{:S(2)}) collective-permute-start(bf16[512,1,128]{0,2,1:T(8,128)(2,1)} %collective-permute-done), channel_id=1, source_target_pairs={{0,16},{16,32},{32,48},{48,64},{64,80},{80,96},{96,112},{112,0},{1... | collective-permute-start | bytes 393224 | tf_op jit(solution)/shard_map/ppermute | solution.py:91
  82.4 6.4 %collective-permute-start.2 = (bf16[512,1,128]{0,2,1:T(8,128)(2,1)S(1)}, bf16[512,1,128]{0,2,1:T(8,128)(2,1)S(1)}, u32[]{:S(2)}, u32[]{:S(2)}) collective-permute-start(bf16[512,1,128]{0,2,1:T(8,128)(2,1)S(1)} %collective-permute-done.1), channel_id=1, source_target_pairs={{0,16},{16,32},{32,48},{48,64},{64,80},{80,96},{96,112},{112,0},{1... | collective-permute-start | bytes 393224 | tf_op jit(solution)/shard_map/ppermute | solution.py:91
  85.1 8.3 %collective-permute-start.5 = (bf16[512,1,128]{0,2,1:T(8,128)(2,1)S(1)}, bf16[512,1,128]{0,2,1:T(8,128)(2,1)S(1)}, u32[]{:S(2)}, u32[]{:S(2)}) collective-permute-start(bf16[512,1,128]{0,2,1:T(8,128)(2,1)S(1)} %collective-permute-done.4), channel_id=1, source_target_pairs={{0,112},{16,0},{32,16},{48,32},{64,48},{80,64},{96,80},{112,96},{1... | collective-permute-start | bytes 393224 | tf_op jit(solution)/shard_map/ppermute | solution.py:93
  88.8 7.2 %collective-permute-start.3 = (bf16[512,1,128]{0,2,1:T(8,128)(2,1)S(1)}, bf16[512,1,128]{0,2,1:T(8,128)(2,1)S(1)}, u32[]{:S(2)}, u32[]{:S(2)}) collective-permute-start(bf16[512,1,128]{0,2,1:T(8,128)(2,1)S(1)} %collective-permute-done.2), channel_id=1, source_target_pairs={{0,16},{16,32},{32,48},{48,64},{64,80},{80,96},{96,112},{112,0},{1... | collective-permute-start | bytes 393224 | tf_op jit(solution)/shard_map/ppermute | solution.py:91
  93.4 8.2 %collective-permute-start.6 = (bf16[512,1,128]{0,2,1:T(8,128)(2,1)S(1)}, bf16[512,1,128]{0,2,1:T(8,128)(2,1)S(1)}, u32[]{:S(2)}, u32[]{:S(2)}) collective-permute-start(bf16[512,1,128]{0,2,1:T(8,128)(2,1)S(1)} %collective-permute-done.5), channel_id=1, source_target_pairs={{0,112},{16,0},{32,16},{48,32},{64,48},{80,64},{96,80},{112,96},{1... | collective-permute-start | bytes 393224 | tf_op jit(solution)/shard_map/ppermute | solution.py:93
  108.7 9.1 %copy-start.6 = (bf16[512,1,2,128]{3,0,2,1:T(8,128)(2,1)S(1)}, bf16[512,1,2,128]{3,0,2,1:T(8,128)(2,1)}, u32[]{:S(2)}) copy-start(bf16[512,1,2,128]{3,0,2,1:T(8,128)(2,1)} %get-tuple-element.122) | copy-start | bytes 786436 | tf_op jit(solution)/shard_map/cond
  117.8 5.5 %copy-start.3 = (pred[512,4096]{0,1:T(8,128)(4,1)S(1)}, pred[512,4096]{0,1:T(8,128)(4,1)}, u32[]{:S(2)}) copy-start(pred[512,4096]{0,1:T(8,128)(4,1)} %compare_and_fusion) | copy-start | bytes 6291460 | tf_op jit(solution)/shard_map/cond
  117.8 5.5 %copy-start.12 = (bf16[4096,1,128]{2,0,1:T(8,128)(2,1)S(1)}, bf16[4096,1,128]{2,0,1:T(8,128)(2,1)}, u32[]{:S(2)}) copy-start(bf16[4096,1,128]{2,0,1:T(8,128)(2,1)} %get-tuple-element.123) | copy-start | bytes 3145732 | tf_op jit(solution)/shard_map/cond
  138.1 74.6 %copy-start.4 = (bf16[32,5376]{1,0:T(8,128)(2,1)S(1)}, bf16[32,5376]{1,0:T(8,128)(2,1)}, u32[]{:S(2)}) copy-start(bf16[32,5376]{1,0:T(8,128)(2,1)} %param.12) | copy-start | bytes 1032196
  138.1 74.7 %copy-start.7 = (f32[5376]{0:T(1024)S(1)}, f32[5376]{0:T(1024)}, u32[]{:S(2)}) copy-start(f32[5376]{0:T(1024)} %param.21) | copy-start | bytes 64516
Sparse Core Ops, SparseCore 0:
  9.2 45.2 all-gather.3
  68.3 38.3 all-gather.5
  138.2 73.2 reduce-scatter.1
